TPU v7x, 512 devices: a whole 4x8x8 slice. The times are simulated.
512 devices in a mesh: segment: 4 (over x), grp: 16 (over y, z_hi), sp: 8 (over z_lo, core).
Axes of the slice: x: 4, y: 8, z: 8 (z_hi: 2, z_lo: 4; z = z_hi * 4 + z_lo), core: 2. Of those that a mesh axis runs over, the one named last changes fastest.
Arguments:
- queries: bfloat16 [4, 16, 4, 32, 16, 2048], P('segment', 'grp', None, 'sp'), may hold values from -140 to 140
- key_states: bfloat16 [4, 16, 4, 32, 16, 2048], P('segment', 'grp', None, 'sp'), may hold values from -6 to 6
- value_states: bfloat16 [4, 16, 4, 32, 16, 2048], P('segment', 'grp', None, 'sp'), may hold values from -6 to 6
- kept_tiles: int32 [16, 8, 4], replicated, may hold values from 0 to 7, as said below
- kept_counts: int32 [16, 8], replicated, may hold values from 1 to 4
- patch_weight: bfloat16 [2048, 64], replicated, may hold values from -1.5 to 1.5
- decode_slot: int32 [4], replicated, may hold values from 0 to 3, each once
- first_kernel: bfloat16 [27, 16, 256], replicated, may hold values from -0.3125 to 0.3125
- second_kernel: bfloat16 [27, 256, 256], P(None, 'grp'), may hold values from -0.078125 to 0.078125
Outputs:
- decoded: bfloat16 [4, 16, 4, 64, 32, 256], P('segment', 'grp', None, 'sp')
Inputs may be any that keep to these rules, and one draw needn't show every extreme that they name: `kept_tiles`: for each head and query tile the 4 entries name distinct tiles, the query tile itself among them in some slot.
All inputs are finite; a program needn't handle non-finite values.
Results may differ from a plain program's by a relative error of at most 0.018.
Values may be sent and summed in bfloat16 or wider, within the bound.
A program may use at most 128 MiB of HBM per device.

v0:
```python
import jax
import jax.numpy as jnp
from jax import lax
from jax.sharding import PartitionSpec as P

HEADS = 16
HD = 128
LAT = 16
CH = 256
TT = 4
TH = 8
TW = 8


VAE_SCALE = 1.0 / 0.476986


def padded_2(cells, sides, width):
    for axis, dim in sides:
        count = lax.axis_size(axis)
        ends = count - 1
        head = lax.slice_in_dim(cells, 0, width, axis=dim)
        tail = lax.slice_in_dim(cells, cells.shape[dim] - width, cells.shape[dim], axis=dim)
        cells = jnp.concatenate(
            [
                lax.ppermute(tail, axis, [(i, (i + 1) % count) for i in range(ends)]),
                cells,
                lax.ppermute(head, axis, [((i + 1) % count, i) for i in range(ends)]),
            ],
            axis=dim,
        )
    return cells


def to_tiles(grid, tile_size):
    frame_count, row_count, col_count, feature_width = grid.shape
    tiled = grid.reshape(
        frame_count // TT, TT, row_count // TH, TH, col_count // TW, TW, feature_width
    ).transpose(0, 2, 4, 1, 3, 5, 6)
    return tiled.reshape(-1, tile_size, feature_width)


def from_tiles(tiles, frame_count, row_count, col_count):
    feature_width = tiles.shape[-1]
    grid = tiles.reshape(
        frame_count // TT, row_count // TH, col_count // TW, TT, TH, TW, feature_width
    ).transpose(0, 3, 1, 4, 2, 5, 6)
    return grid.reshape(frame_count, row_count, col_count, feature_width)


def attend_tiles(query_tiles, key_tiles, value_tiles, tile_index, live_count):
    head_count = query_tiles.shape[0]
    tile_size = query_tiles.shape[2]
    head_size = query_tiles.shape[3]
    keep_count = tile_index.shape[2]

    def one_tile(packed):
        query_block, index_block, count_block = packed
        key_sel = jax.vmap(lambda source, picks: source[picks])(key_tiles, index_block).reshape(
            head_count, keep_count * tile_size, head_size
        )
        value_sel = jax.vmap(lambda source, picks: source[picks])(value_tiles, index_block).reshape(
            head_count, keep_count * tile_size, head_size
        )
        scores = jnp.einsum(
            "hqd,hkd->hqk", query_block, key_sel, preferred_element_type=jnp.float32
        ) * head_size ** (-0.5)
        live = jnp.arange(keep_count, dtype=jnp.int32)[None, :] < count_block[:, None]
        live = jnp.repeat(live, tile_size, axis=1)[:, None, :]
        scores = jnp.where(live, scores, -1e30)
        row_top = jnp.max(scores, axis=-1, keepdims=True)
        exponent = jnp.where(live, jnp.exp(scores - row_top), 0.0)
        weights = (exponent / jnp.sum(exponent, axis=-1, keepdims=True)).astype(jnp.bfloat16)
        result = jnp.einsum("hqk,hkd->hqd", weights, value_sel, preferred_element_type=jnp.float32)
        return result.astype(jnp.bfloat16)

    return lax.map(
        one_tile,
        (
            query_tiles.transpose(1, 0, 2, 3),
            tile_index.transpose(1, 0, 2),
            live_count.transpose(1, 0),
        ),
    )


def edge_fill(padded, axis_dim, depth, at_first, at_last):
    extent = padded.shape[axis_dim]
    inner_first = lax.slice_in_dim(padded, depth, depth + 1, axis=axis_dim)
    inner_last = lax.slice_in_dim(padded, extent - depth - 1, extent - depth, axis=axis_dim)
    position = lax.broadcasted_iota(jnp.int32, padded.shape, axis_dim)
    padded = jnp.where(jnp.logical_and(at_first, position < depth), inner_first, padded)
    padded = jnp.where(jnp.logical_and(at_last, position >= extent - depth), inner_last, padded)
    return padded


def pad_columns(block, depth):
    return jnp.pad(block, ((0, 0), (0, 0), (0, 0), (depth, depth), (0, 0)))


def causal_pad(block):
    first_frame = block[:, :1]
    return jnp.concatenate([first_frame, first_frame, block], axis=1)


def window_columns(padded, row_count, col_count):
    frame_count = padded.shape[1] - 2
    pieces = []
    for offset_time in range(3):
        for offset_row in range(3):
            for offset_col in range(3):
                pieces.append(
                    padded[
                        :,
                        offset_time : offset_time + frame_count,
                        offset_row : offset_row + row_count,
                        offset_col : offset_col + col_count,
                    ]
                )
    stacked = jnp.stack(pieces, axis=-2)
    return stacked.reshape(-1, 27, padded.shape[-1])


def first_conv(rimmed, kernel, row_count, col_count):
    columns = window_columns(causal_pad(rimmed), row_count, col_count).reshape(
        -1, kernel.shape[0] * kernel.shape[1]
    )
    flat_kernel = kernel.reshape(-1, kernel.shape[2])
    result = jnp.dot(columns, flat_kernel, preferred_element_type=jnp.float32) * VAE_SCALE
    return result.astype(jnp.bfloat16).reshape(
        rimmed.shape[0], rimmed.shape[1] - 0, row_count, col_count, kernel.shape[2]
    )


def local(
    queries,
    key_states,
    value_states,
    kept_tiles,
    kept_counts,
    patch_weight,
    decode_slot,
    first_kernel,
    second_kernel,
):
    frame_count = queries.shape[2]
    local_rows = queries.shape[3]
    token_cols = queries.shape[4]
    feature_count = queries.shape[5]
    tokens = frame_count * local_rows * token_cols
    sp_count = lax.axis_size("sp")
    sp_rank = lax.axis_index("sp")
    local_heads = HEADS // sp_count
    clip_rows = local_rows * sp_count
    tile_size = TT * TH * TW
    flat_query = queries.reshape(tokens, feature_count)
    flat_key = key_states.reshape(tokens, feature_count)
    flat_value = value_states.reshape(tokens, feature_count)
    mixed_query, mixed_key, mixed_value = (
        lax.all_to_all(flat_query, "sp", split_axis=1, concat_axis=0, tiled=True),
        lax.all_to_all(flat_key, "sp", split_axis=1, concat_axis=0, tiled=True),
        lax.all_to_all(flat_value, "sp", split_axis=1, concat_axis=0, tiled=True),
    )
    own_width = mixed_query.shape[1]

    def head_tiles(mixed):
        grid = mixed.reshape(sp_count, frame_count, local_rows, token_cols, own_width).transpose(
            1, 0, 2, 3, 4
        )
        tiles = to_tiles(grid.reshape(frame_count, clip_rows, token_cols, own_width), tile_size)
        return tiles.reshape(tiles.shape[0], tile_size, local_heads, HD).transpose(2, 0, 1, 3)

    own_tiles = lax.dynamic_slice_in_dim(kept_tiles, sp_rank * local_heads, local_heads, 0)
    own_counts = lax.dynamic_slice_in_dim(kept_counts, sp_rank * local_heads, local_heads, 0)
    outputs = attend_tiles(
        head_tiles(mixed_query),
        head_tiles(mixed_key),
        head_tiles(mixed_value),
        own_tiles,
        own_counts,
    )
    tile_count = outputs.shape[0]
    attended = from_tiles(
        outputs.transpose(0, 2, 1, 3).reshape(tile_count, tile_size, own_width),
        frame_count,
        clip_rows,
        token_cols,
    )
    attended = attended.reshape(frame_count, sp_count, local_rows, token_cols, own_width).transpose(
        1, 0, 2, 3, 4
    )
    attended = attended.reshape(sp_count * tokens, own_width)
    restored = lax.all_to_all(attended, "sp", split_axis=0, concat_axis=1, tiled=True)
    latent = jnp.dot(restored, patch_weight, preferred_element_type=jnp.float32)
    latent = latent.astype(jnp.bfloat16)
    segment_count = lax.axis_size("segment")
    segment_rank = lax.axis_index("segment")
    every_segment = lax.all_gather(latent[None], "segment", axis=0, tiled=True)
    picks = (decode_slot == segment_rank).astype(jnp.int32)
    source = jnp.sum(jnp.arange(segment_count, dtype=jnp.int32) * picks)
    chosen = lax.dynamic_index_in_dim(every_segment, source, 0, keepdims=False)
    cells = chosen.reshape(frame_count, local_rows, token_cols, 2, 2, LAT).transpose(
        0, 1, 3, 2, 4, 5
    )
    cells = cells.reshape(1, frame_count, 2 * local_rows, 2 * token_cols, LAT)
    row_count = 2 * local_rows
    col_count = 2 * token_cols
    sp_first = sp_rank == 0
    sp_last = sp_rank == sp_count - 1

    def boundary(block, depth):
        block = edge_fill(block, 2, depth, sp_first, sp_last)
        return edge_fill(block, 3, depth, True, True)

    rimmed = padded_2(cells, (("sp", 2),), 1)
    first = first_conv(boundary(pad_columns(rimmed, 1), 1), first_kernel, row_count, col_count)
    act = jax.nn.silu(first.astype(jnp.float32)).astype(jnp.bfloat16)
    act_rim = padded_2(act, (("sp", 2),), 1)
    act_rim = boundary(pad_columns(act_rim, 1), 1)
    columns = window_columns(causal_pad(act_rim), row_count, col_count)
    cell_count = columns.shape[0]
    second = lax.dot_general(
        columns,
        lax.all_gather(second_kernel, "grp", axis=1, tiled=True),
        (((1, 2), (0, 1)), ((), ())),
        preferred_element_type=jnp.float32,
    )
    summed = first.astype(jnp.float32).reshape(cell_count, CH) + second
    return summed.astype(jnp.bfloat16).reshape(1, 1, frame_count, row_count, col_count, CH)


def solution(mesh):
    return jax.shard_map(
        local,
        mesh=mesh,
        in_specs=(
            P("segment", "grp", None, "sp", None, None),
            P("segment", "grp", None, "sp", None, None),
            P("segment", "grp", None, "sp", None, None),
            P(),
            P(),
            P(),
            P(),
            P(),
            P(None, "grp", None),
        ),
        out_specs=P("segment", "grp", None, "sp", None, None),
        check_vma=False,
    )
```

profile of v0, /device:TPU:8, one launch (start us, length us, event | category | flops | bytes accessed | tf_op | source)
XLA Modules:
  0.0 331.0 jit_solution(11924554840574110593)
XLA Ops:
  9.4 7.4 %all-to-all-start = ((bf16[256,8,256]{2,0,1:T(8,128)(2,1)}), bf16[256,8,256]{2,0,1:T(8,128)(2,1)S(1)}, u32[]{:S(2)}, u32[]{:S(2)}) async-start(bf16[256,8,256]{2,0,1:T(8,128)(2,1)} %copy.290), calls=%async_computation | async-start | bytes 2097152 | tf_op jit(solution)/shard_map/all_to_all | solution.py:160
  19.5 23.9 %all-to-all-done = bf16[256,8,256]{2,0,1:T(8,128)(2,1)S(1)} async-done(((bf16[256,8,256]{2,0,1:T(8,128)(2,1)}), bf16[256,8,256]{2,0,1:T(8,128)(2,1)S(1)}, u32[]{:S(2)}, u32[]{:S(2)}) %all-to-all-start) | async-done | bytes 1048608 | tf_op jit(solution)/shard_map/all_to_all | solution.py:160
  43.4 3.6 %all-to-all-start.1 = ((bf16[256,8,256]{2,0,1:T(8,128)(2,1)}), bf16[256,8,256]{2,0,1:T(8,128)(2,1)S(1)}, u32[]{:S(2)}, u32[]{:S(2)}) async-start(bf16[256,8,256]{2,0,1:T(8,128)(2,1)} %copy.294), calls=%async_computation.1 | async-start | bytes 2097152 | tf_op jit(solution)/shard_map/all_to_all | solution.py:161
  48.5 25.0 %all-to-all-done.1 = bf16[256,8,256]{2,0,1:T(8,128)(2,1)S(1)} async-done(((bf16[256,8,256]{2,0,1:T(8,128)(2,1)}), bf16[256,8,256]{2,0,1:T(8,128)(2,1)S(1)}, u32[]{:S(2)}, u32[]{:S(2)}) %all-to-all-start.1) | async-done | bytes 1048608 | tf_op jit(solution)/shard_map/all_to_all | solution.py:161
  73.5 3.6 %all-to-all-start.2 = ((bf16[256,8,256]{2,0,1:T(8,128)(2,1)}), bf16[256,8,256]{2,0,1:T(8,128)(2,1)S(1)}, u32[]{:S(2)}, u32[]{:S(2)}) async-start(bf16[256,8,256]{2,0,1:T(8,128)(2,1)} %copy.297), calls=%async_computation.2 | async-start | bytes 2097152 | tf_op jit(solution)/shard_map/all_to_all | solution.py:162
  79.5 24.1 %all-to-all-done.2 = bf16[256,8,256]{2,0,1:T(8,128)(2,1)S(1)} async-done(((bf16[256,8,256]{2,0,1:T(8,128)(2,1)}), bf16[256,8,256]{2,0,1:T(8,128)(2,1)S(1)}, u32[]{:S(2)}, u32[]{:S(2)}) %all-to-all-start.2) | async-done | bytes 1048608 | tf_op jit(solution)/shard_map/all_to_all | solution.py:162
  106.4 60.1 %while.10 = (s32[]{:T(128)}, bf16[8,2,256,128]{3,2,1,0:T(8,128)(2,1)}, s32[8,2]{1,0:T(8,128)S(1)}, bf16[8,2,256,128]{3,1,2,0:T(2,128)(2,1)}, s32[8,2,4]{2,1,0:T(...) while((s32[]{:T(128)}, ...), condition=%wide.region_3.4_spmd, body=%wide.region_0.3_spmd.sunk | while | flops 272172096 | bytes 7877581 | solution.py:77
  109.0 2.1 fusion.110
  111.2 2.7 fusion.111
  116.5 2.1 fusion.110
  118.7 2.8 fusion.111
  124.0 2.1 fusion.110
  126.2 2.7 fusion.111
  133.7 2.7 fusion.111
  139.0 2.1 fusion.110
  141.2 2.7 fusion.111
  146.6 2.1 fusion.110
  148.7 2.7 fusion.111
  154.1 2.1 fusion.110
  156.2 2.7 fusion.111
  161.6 2.1 fusion.110
  163.7 2.7 fusion.111
  166.5 2.3 copy.303
  170.7 3.6 %all-to-all-start.3 = ((bf16[8,256,256]{2,1,0:T(8,128)(2,1)}), bf16[8,256,256]{2,1,0:T(8,128)(2,1)S(1)}, u32[]{:S(2)}, u32[]{:S(2)}) async-start(bf16[8,256,256]{2,1,0:T(8,128)(2,1)} %bitcast.30), calls=%async_computation.3 | async-start | bytes 2097152 | tf_op jit(solution)/shard_map/all_to_all | solution.py:193
  177.6 23.3 %all-to-all-done.3 = bf16[8,256,256]{2,1,0:T(8,128)(2,1)S(1)} async-done(((bf16[8,256,256]{2,1,0:T(8,128)(2,1)}), bf16[8,256,256]{2,1,0:T(8,128)(2,1)S(1)}, u32[]{:S(2)}, u32[]{:S(2)}) %all-to-all-start.3) | async-done | bytes 1048608 | tf_op jit(solution)/shard_map/all_to_all | solution.py:193
  201.7 12.3 %all-gather = bf16[1024,64]{0,1:T(8,128)(2,1)S(1)} all-gather(bf16[256,64]{0,1:T(8,128)(2,1)S(1)} %convolution_convert_fusion.1), channel_id=2, replica_groups=mesh['segment'=4,'grp'=16,'sp'=8] {'segment'}, dimensions={0}, use_global_device_ids=true | all-gather | bytes 163840 | tf_op jit(solution)/shard_map/all_gather | solution.py:198
  216.1 3.2 collective-permute-start
  242.1 9.3 %copy.313 = bf16[1,4,8,32,27,16]{3,2,1,5,4,0:T(8,128)(2,1)} copy(bf16[1,4,8,32,27,16]{5,3,2,1,4,0:T(8,128)(2,1)} %fusion.64) | data formatting | bytes 1769472 | tf_op jit(solution)/shard_map/stack | solution.py:120
  251.4 5.3 %reshape_reshape.35 = bf16[1024,432]{0,1:T(8,128)(2,1)S(1)} reshape(bf16[1,4,8,32,27,16]{3,2,1,5,4,0:T(8,128)(2,1)} %copy.313) | data formatting | bytes 1769472 | tf_op jit(solution)/shard_map/reshape;reshape | solution.py:125
  258.9 3.4 %collective-permute-start.2 = (bf16[1,4,1,32,256]{4,3,2,1,0:T(8,128)(2,1)S(1)}, bf16[1,4,1,32,256]{4,3,2,1,0:T(8,128)(2,1)S(1)}, u32[]{:S(2)}, u32[]{:S(2)}) collective-permute-start(bf16[1,4,1,32,256]{4,3,2,1,0:T(8,128)(2,1)S(1)} %get-tuple-element.132), channel_id=1, source_target_pairs={{0,1},{1,2},{2,3},{3,4},{4,5},{5,6},{6,7},{8,9},{9,10},{10,11},{11... | collective-permute-start | bytes 196616 | tf_op jit(solution)/shard_map/ppermute | solution.py:26
  290.5 23.0 %all-gather.3.cloned.1.call-done = bf16[27,256,256]{2,1,0:T(8,128)(2,1)} async-done(((bf16[27,16,256]{2,1,0:T(8,128)(2,1)}), bf16[27,256,256]{2,1,0:T(8,128)(2,1)}) %all-gather.3.cloned.1.call-update) | async-done | bytes 3538960 | tf_op jit(solution)/shard_map/all_gather | solution.py:224
  313.5 10.6 %fusion.20 = bf16[1024,256]{1,0:T(8,128)(2,1)} fusion(f32[1024,256]{1,0:T(8,128)S(1)} %fusion.19, bf16[1024,27,256]{2,0,1:T(8,128)(2,1)} %constant_dynamic-update-slice_fusion, bf16[27,256,256]{2,1,0:T(8,128)(2,1)} %all-gather.3.cloned.1.call-done), kind=kOutput, calls=%fused_computation.51 | convolution fusion | flops 3624402944 | bytes 19267584 | tf_op jit(solution)/shard_map/dot_general | solution.py:222
  (242 shorter events, 93.9 us)
Async XLA Ops:
  6.5 194.9 %copy-start = (bf16[2048,64]{0,1:T(8,128)(2,1)S(1)}, bf16[2048,64]{0,1:T(8,128)(2,1)}, u32[]{:S(2)}) copy-start(bf16[2048,64]{0,1:T(8,128)(2,1)} %param.16) | copy-start | bytes 786436
  6.5 40.4 %copy-start.1 = (bf16[1,1,4,4,16,2048]{5,4,3,2,1,0:T(8,128)(2,1)S(1)}, bf16[1,1,4,4,16,2048]{5,4,3,2,1,0:T(8,128)(2,1)}, u32[]{:S(2)}) copy-start(bf16[1,1,4,4,16,2048]{5,4,3,2,1,0:T(8,128)(2,1)} %param.13) | copy-start | bytes 3145732
  9.4 67.7 %copy-start.2 = (s32[16,8,4]{0,2,1:T(4,128)S(1)}, s32[16,8,4]{0,2,1:T(4,128)}, u32[]{:S(2)}) copy-start(s32[16,8,4]{0,2,1:T(4,128)} %param.14) | copy-start | bytes 6148
  9.4 67.9 %copy-start.3 = (s32[16,8]{0,1:T(8,128)S(1)}, s32[16,8]{0,1:T(8,128)}, u32[]{:S(2)}) copy-start(s32[16,8]{0,1:T(8,128)} %param.15) | copy-start | bytes 1540
  9.4 34.0 %all-to-all-start = ((bf16[256,8,256]{2,0,1:T(8,128)(2,1)}), bf16[256,8,256]{2,0,1:T(8,128)(2,1)S(1)}, u32[]{:S(2)}, u32[]{:S(2)}) async-start(bf16[256,8,256]{2,0,1:T(8,128)(2,1)} %copy.290), calls=%async_computation | async-start | bytes 2097152 | tf_op jit(solution)/shard_map/all_to_all | solution.py:160
  43.4 30.1 %all-to-all-start.1 = ((bf16[256,8,256]{2,0,1:T(8,128)(2,1)}), bf16[256,8,256]{2,0,1:T(8,128)(2,1)S(1)}, u32[]{:S(2)}, u32[]{:S(2)}) async-start(bf16[256,8,256]{2,0,1:T(8,128)(2,1)} %copy.294), calls=%async_computation.1 | async-start | bytes 2097152 | tf_op jit(solution)/shard_map/all_to_all | solution.py:161
  73.5 30.1 %all-to-all-start.2 = ((bf16[256,8,256]{2,0,1:T(8,128)(2,1)}), bf16[256,8,256]{2,0,1:T(8,128)(2,1)S(1)}, u32[]{:S(2)}, u32[]{:S(2)}) async-start(bf16[256,8,256]{2,0,1:T(8,128)(2,1)} %copy.297), calls=%async_computation.2 | async-start | bytes 2097152 | tf_op jit(solution)/shard_map/all_to_all | solution.py:162
  106.4 1.0 copy-start.4
  111.2 2.7 copy-start.5
  113.9 0.9 copy-start.4
  118.7 2.8 copy-start.5
  121.4 0.9 copy-start.4
  126.2 2.8 copy-start.5
  128.9 0.9 copy-start.4
  133.7 2.8 copy-start.5
  136.4 0.9 copy-start.4
  141.2 2.8 copy-start.5
  143.9 0.9 copy-start.4
  148.7 2.7 copy-start.5
  151.4 0.9 copy-start.4
  156.2 2.8 copy-start.5
  159.0 0.9 copy-start.4
  163.7 2.8 copy-start.5
  166.5 8.5 %copy-start.7 = (s32[4]{0:T(128)S(1)}, s32[4]{0:T(128)}, u32[]{:S(2)}) copy-start(s32[4]{0:T(128)} %param.17) | copy-start | bytes 52
  170.7 30.2 %all-to-all-start.3 = ((bf16[8,256,256]{2,1,0:T(8,128)(2,1)}), bf16[8,256,256]{2,1,0:T(8,128)(2,1)S(1)}, u32[]{:S(2)}, u32[]{:S(2)}) async-start(bf16[8,256,256]{2,1,0:T(8,128)(2,1)} %bitcast.30), calls=%async_computation.3 | async-start | bytes 2097152 | tf_op jit(solution)/shard_map/all_to_all | solution.py:193
  174.3 139.3 %all-gather.3.cloned.1.call-start = ((), (), s32[]{:S(2)}) async-start(), calls=%async_computation.4 | async-start | bytes 3760128 | tf_op jit(solution)/shard_map/all_gather | solution.py:224
  214.8 4.5 %collective-permute-start.1 = (bf16[1,4,1,32,16]{4,3,2,1,0:T(8,128)(2,1)S(1)}, bf16[1,4,1,32,16]{4,3,2,1,0:T(8,128)(2,1)S(1)}, u32[]{:S(2)}, u32[]{:S(2)}) collective-permute-start(bf16[1,4,1,32,16]{4,3,2,1,0:T(8,128)(2,1)S(1)} %get-tuple-element.139), channel_id=1, source_target_pairs={{1,0},{2,1},{3,2},{4,3},{5,4},{6,5},{7,6},{9,8},{10,9},{11,10},{12... | collective-permute-start | bytes 12296 | tf_op jit(solution)/shard_map/ppermute | solution.py:28
  216.1 3.9 %collective-permute-start = (bf16[1,4,1,32,16]{4,3,2,1,0:T(8,128)(2,1)S(1)}, bf16[1,4,1,32,16]{4,3,2,1,0:T(8,128)(2,1)S(1)}, u32[]{:S(2)}, u32[]{:S(2)}) collective-permute-start(bf16[1,4,1,32,16]{4,3,2,1,0:T(8,128)(2,1)S(1)} %get-tuple-element.138), channel_id=1, source_target_pairs={{0,1},{1,2},{2,3},{3,4},{4,5},{5,6},{6,7},{8,9},{9,10},{10,11},{11... | collective-permute-start | bytes 12296 | tf_op jit(solution)/shard_map/ppermute | solution.py:26
  242.1 14.7 %copy-start.6 = (bf16[27,16,256]{2,1,0:T(8,128)(2,1)S(1)}, bf16[27,16,256]{2,1,0:T(8,128)(2,1)}, u32[]{:S(2)}) copy-start(bf16[27,16,256]{2,1,0:T(8,128)(2,1)} %param.18) | copy-start | bytes 663556
  257.6 4.7 %collective-permute-start.3 = (bf16[1,4,1,32,256]{4,3,2,1,0:T(8,128)(2,1)S(1)}, bf16[1,4,1,32,256]{4,3,2,1,0:T(8,128)(2,1)S(1)}, u32[]{:S(2)}, u32[]{:S(2)}) collective-permute-start(bf16[1,4,1,32,256]{4,3,2,1,0:T(8,128)(2,1)S(1)} %get-tuple-element.133), channel_id=1, source_target_pairs={{1,0},{2,1},{3,2},{4,3},{5,4},{6,5},{7,6},{9,8},{10,9},{11,10},{12... | collective-permute-start | bytes 196616 | tf_op jit(solution)/shard_map/ppermute | solution.py:28
  258.9 4.0 %collective-permute-start.2 = (bf16[1,4,1,32,256]{4,3,2,1,0:T(8,128)(2,1)S(1)}, bf16[1,4,1,32,256]{4,3,2,1,0:T(8,128)(2,1)S(1)}, u32[]{:S(2)}, u32[]{:S(2)}) collective-permute-start(bf16[1,4,1,32,256]{4,3,2,1,0:T(8,128)(2,1)S(1)} %get-tuple-element.132), channel_id=1, source_target_pairs={{0,1},{1,2},{2,3},{3,4},{4,5},{5,6},{6,7},{8,9},{9,10},{10,11},{11... | collective-permute-start | bytes 196616 | tf_op jit(solution)/shard_map/ppermute | solution.py:26
Sparse Core Ops, SparseCore 0:
  178.1 135.3 all-gather.2
where the time goes:
time: 332 us; the launch traced here: 331 us
  waiting for transfers between devices  121 us (36%)
  local copies, waits for them, and re-layouts  90.1 us (27%)
  matrix products  50.6 us (15%)
  starting transfers between devices  27.3 us (8%)
  between operations  15.9 us (5%)
  other arithmetic  13.2 us (4%)
  blocking collectives  12.3 us (4%)
    unnamed x60, local copies, waits for them, and re-layouts  38.4 us
    all_to_all x1, waiting for transfers between devices, local(): lax.all_to_all(flat_key, 'sp', split_axis=1, concat_axis=0, tiled=True)  25 us
    all_to_all x1, waiting for transfers between devices, local(): lax.all_to_all(flat_value, 'sp', split_axis=1, concat_axis=0, tiled=True)  24.1 us
    all_to_all x1, waiting for transfers between devices, local(): lax.all_to_all(flat_query, 'sp', split_axis=1, concat_axis=0, tiled=True)  23.9 us
    all_to_all x1, waiting for transfers between devices, local(): lax.all_to_all(attended, 'sp', split_axis=0, concat_axis=1, tiled=True)  23.3 us
    all_gather x1, waiting for transfers between devices, local(): lax.all_gather(second_kernel, 'grp', axis=1, tiled=True)  23 us
    dot_general x8, matrix products, one_tile(): jnp.einsum('hqk,hkd->hqd', weights, value_sel, preferred_element_type=jnp...  22 us
    sub x8, matrix products, one_tile(): exponent = jnp.where(live, jnp.exp(scores - row_top), 0.0)  17.2 us
  transfers between devices with their start and end apart: 9, of which 7 were waited for; matrix products, arithmetic and copies ran while one was open for 22% of the time, Pallas kernels for 0%

commit v1 on v0

v1 whole, which is shorter than its diff:
```python
import functools
import math

import jax
import jax.numpy as jnp
from jax import lax
from jax.experimental import pallas as pl
from jax.experimental.pallas import tpu as pltpu
from jax.sharding import PartitionSpec as P

HEADS = 16
HD = 128
LAT = 16
CH = 256
NT = 8
KEEP = 4
TILE = 256
VAE_SCALE = 1.0 / 0.476986
MESH = pl.DeviceIdType.MESH
BF16 = jnp.bfloat16
F32 = jnp.float32
EXPONENT_SCALE = HD**-0.5 * math.log2(math.e)


def remote(src, dst, send_sem, recv_sem, **where):
    return pltpu.make_async_remote_copy(
        src_ref=src,
        dst_ref=dst,
        send_sem=send_sem,
        recv_sem=recv_sem,
        device_id=where,
        device_id_type=MESH,
    )


def exchange_kernel(
    kept,
    counts,
    decode_slot,
    queries,
    keys,
    values,
    patch,
    piece,
    latent_out,
    weights_out,
    got_q,
    got_k,
    got_v,
    tile_q,
    tile_k,
    tile_v,
    order,
    patch_own,
    attended,
    part_out,
    part_in,
    seg_latent,
    send_sem,
    recv_sem,
    local_sem,
    part_send,
    part_recv,
    seg_send,
    seg_recv,
    w_local,
    w_send,
    w_recv,
):
    me = lax.axis_index("sp")
    seg = lax.axis_index("segment")
    grp = lax.axis_index("grp")
    chip = me // 2
    core = me % 2
    sibling = chip * 2 + 1 - core
    far = (chip + 2) % 4
    mirror = 3 - chip
    near = chip + 1 - 2 * (chip % 2)
    peers = [
        far * 2 + core,
        far * 2 + 1 - core,
        mirror * 2 + core,
        mirror * 2 + 1 - core,
        near * 2 + core,
        near * 2 + 1 - core,
        sibling,
    ]
    z_partner = grp + 1 - 2 * (grp % 2)
    y_peers = [(grp + 2 * step) % 16 for step in range(1, 8)]
    x_peers = [(seg + step) % 4 for step in range(1, 4)]

    barrier = pltpu.get_barrier_semaphore()
    for peer in peers:
        pl.semaphore_signal(barrier, inc=1, device_id={"sp": peer}, device_id_type=MESH)
    for peer in x_peers:
        pl.semaphore_signal(barrier, inc=1, device_id={"segment": peer}, device_id_type=MESH)
    for peer in [z_partner] + y_peers:
        pl.semaphore_signal(barrier, inc=1, device_id={"grp": peer}, device_id_type=MESH)
    pl.semaphore_wait(barrier, 18)

    quarter = seg * 7
    taps = pl.ds(quarter, 7)
    lanes = pl.ds(pl.multiple_of(core * 128, 128), 128)
    own_part = piece.at[pl.ds(quarter - seg // 3, 7), :, lanes]
    own_rows = pl.ds(pl.multiple_of(grp * 16, 16), 16)
    w_keep = pltpu.make_async_copy(own_part, weights_out.at[taps, own_rows, lanes], w_local)
    w_keep.start()
    w_cross = remote(
        own_part, weights_out.at[taps, own_rows, lanes], w_send.at[0], w_recv.at[0], grp=z_partner
    )
    w_cross.start()

    arrays = ((keys, got_k), (values, got_v), (queries, got_q))
    sends = []
    for a, (source, target) in enumerate(arrays):
        for i, peer in enumerate(peers):
            columns = pl.ds(pl.multiple_of(peer * 256, 256), 256)
            copy = remote(
                source.at[:, columns],
                target.at[me],
                send_sem.at[a, i],
                recv_sem.at[a, me],
                sp=peer,
            )
            copy.start()
            sends.append(copy)
    own_columns = pl.ds(pl.multiple_of(me * 256, 256), 256)
    keeps = []
    for a, (source, target) in enumerate(arrays):
        copy = pltpu.make_async_copy(source.at[:, own_columns], target.at[me], local_sem.at[a])
        copy.start()
        keeps.append(copy)
    patch_copy = pltpu.make_async_copy(
        patch.at[:, pl.ds(pl.multiple_of(me * 256, 256), 256)], patch_own, local_sem.at[3]
    )
    patch_copy.start()

    w_keep.wait()
    w_cross.wait()
    pair_rows = pl.ds(pl.multiple_of((grp // 2) * 32, 32), 32)
    y_sends = []
    for i, peer in enumerate(y_peers):
        block = weights_out.at[taps, pair_rows, lanes]
        copy = remote(block, block, w_send.at[1 + i], w_recv.at[1 + i], grp=peer)
        copy.start()
        y_sends.append(copy)
    for copy in keeps:
        copy.wait()
    patch_copy.wait()
    for copy in y_sends:
        copy.wait()
    x_sends = []
    own_quarter = weights_out.at[taps, :, lanes]
    for i, peer in enumerate(x_peers):
        copy = remote(own_quarter, own_quarter, w_send.at[8 + i], w_recv.at[8 + i], segment=peer)
        copy.start()
        x_sends.append(copy)

    def wait_block(a, target, src):
        remote(
            target.at[src], target.at[src], send_sem.at[a, 0], recv_sem.at[a, src], sp=sibling
        ).wait_recv()

    to_row = lax.broadcasted_iota(jnp.int32, (256, 256), 0)
    from_row = lax.broadcasted_iota(jnp.int32, (256, 256), 1)
    wanted = ((to_row % 128) // 8) * 16 + (to_row // 128) * 8 + to_row % 8
    order[...] = (from_row == wanted).astype(BF16)

    def place(got, src, tiles, first_tile):
        block = jnp.dot(order[...], got[src], preferred_element_type=F32).astype(BF16)
        rows = pl.ds(pl.multiple_of((src % 2) * 128, 128), 128)
        for head in range(2):
            for side in range(2):
                tiles[head, first_tile + side, rows] = block[
                    side * 128 : side * 128 + 128, head * 128 : head * 128 + 128
                ]

    def place_keys(src):
        place(got_k, src, tile_k, 2 * (src // 2))
        place(got_v, src, tile_v, 2 * (src // 2))

    place_keys(me)
    for peer in (peers[6], peers[4], peers[5]):
        wait_block(0, got_k, peer)
        wait_block(1, got_v, peer)
        place_keys(peer)

    for copy in x_sends:
        copy.wait()
    all_lanes = weights_out.at[:, :, lanes]
    to_sibling = remote(all_lanes, all_lanes, w_send.at[11], w_recv.at[11], sp=sibling)
    to_sibling.start()

    for peer in peers[:4]:
        wait_block(0, got_k, peer)
        wait_block(1, got_v, peer)
        place_keys(peer)

    head_base = me * 2
    zero_patch = jnp.zeros((64, 256), F32)
    own_patch = patch_own[...].astype(F32)
    wide_patch = jnp.concatenate(
        [
            jnp.concatenate([own_patch, zero_patch], axis=1),
            jnp.concatenate([zero_patch, own_patch], axis=1),
        ],
        axis=0,
    ).astype(BF16)

    def one_tile(owner, side):
        tile = 2 * owner + side
        for head in range(2):
            low = head * 128
            query = tile_q[head, side]
            live = counts[tile, head_base + head]
            scores, picks = [], []
            for slot in range(KEEP):
                pick = kept[tile, slot, head_base + head]
                picks.append(pick)
                scores.append(
                    lax.dot_general(
                        query,
                        tile_k[head, pick],
                        (((1,), (1,)), ((), ())),
                        preferred_element_type=F32,
                    )
                )
            top = scores[0]
            for slot in range(1, KEEP):
                top = jnp.maximum(top, jnp.where(slot < live, scores[slot], -1e30))
            top = jnp.max(top, axis=1, keepdims=True) * EXPONENT_SCALE
            total = jnp.zeros((TILE, TILE), F32)
            result = jnp.zeros((TILE, HD), F32)
            for slot in range(KEEP):
                shift = top if slot == 0 else jnp.where(slot < live, top, 1e30)
                exponent = jnp.exp2(scores[slot] * EXPONENT_SCALE - shift)
                total = total + exponent
                result = result + jnp.dot(
                    exponent.astype(BF16), tile_v[head, picks[slot]], preferred_element_type=F32
                )
            total = jnp.sum(total, axis=1, keepdims=True)
            attended[side, :, low : low + 128] = (result / total).astype(BF16)

    def part_targets(owner, half):
        block = 2 * owner + half
        last = block // 7
        start = 1 - (block + 6) // 7
        own = part_out.at[owner, half]
        return (
            (own, block, 32, 128),
            (own.at[pl.ds(96, 32)], block + 1 - last, 160 * last, 32),
            (own.at[pl.ds(0, 32)], block - 1 + start, 160 * (1 - start), 32),
        )

    def one_chip(owner):
        place(got_q, 2 * owner, tile_q, 0)
        place(got_q, 2 * owner + 1, tile_q, 0)
        one_tile(owner, 0)
        one_tile(owner, 1)
        stacked = []
        for half in range(2):
            for side in range(2):
                base = half * 128
                stacked.append(
                    jnp.concatenate(
                        [
                            attended[side, base : base + 64],
                            attended[side, base + 64 : base + 128],
                        ],
                        axis=1,
                    )
                )
        projected = lax.dot_general(
            jnp.concatenate(stacked, axis=0),
            wide_patch,
            (((1,), (1,)), ((), ())),
            preferred_element_type=F32,
        )
        for half in range(2):
            pieces = []
            for row in range(4):
                for frame in range(2):
                    for side in range(2):
                        at = ((half * 2 + side) * 8 + frame * 4 + row) * 8
                        pieces.append(projected[at : at + 8])
            part_out[owner, half] = jnp.concatenate(pieces, axis=0).astype(BF16)
        for half in range(2):
            for kind, (source, target, at, size) in enumerate(part_targets(owner, half)):
                place_at = part_in.at[me, pl.ds(pl.multiple_of(at, 32), size)]

                @pl.when(target != me)
                def _():
                    remote(
                        source,
                        place_at,
                        part_send.at[owner, half, kind],
                        part_recv.at[me],
                        sp=target,
                    ).start()

                @pl.when(target == me)
                def _():
                    pltpu.make_async_copy(source, place_at, part_recv.at[me]).start()

    def chip_turn(turn, carry):
        owner = (
            (turn == 0) * chip + (turn == 1) * near + (turn == 2) * far + (turn == 3) * mirror
        )

        @pl.when(turn > 0)
        def _():
            for k in range(2):
                wait_block(2, got_q, owner * 2 + k)

        one_chip(owner)
        return carry

    wait_block(2, got_q, sibling)
    lax.fori_loop(0, 4, chip_turn, 0)

    for src in range(8):
        pltpu.make_async_copy(part_in.at[src], part_in.at[src], part_recv.at[src]).wait()
    latent = jnp.zeros((192, 128), F32)
    for src in range(8):
        latent = latent + part_in[src].astype(F32)
    seg_latent[seg] = latent.astype(BF16)
    seg_copies = []
    for i, peer in enumerate(x_peers):
        copy = remote(
            seg_latent.at[seg], seg_latent.at[seg], seg_send.at[i], seg_recv.at[i], segment=peer
        )
        copy.start()
        seg_copies.append(copy)
    for copy in seg_copies:
        copy.wait()
    source = jnp.int32(0)
    for micro in range(1, 4):
        source = jnp.where(decode_slot[micro] == seg, micro, source)
    latent_out[...] = seg_latent[source]

    def drain(owner, carry):
        for half in range(2):
            for kind, (source, target, at, size) in enumerate(part_targets(owner, half)):

                @pl.when(target != me)
                def _():
                    remote(
                        source,
                        part_in.at[me, pl.ds(0, size)],
                        part_send.at[owner, half, kind],
                        part_recv.at[me],
                        sp=target,
                    ).wait_send()

        return carry

    lax.fori_loop(0, 4, drain, 0)
    to_sibling.wait()
    for copy in sends:
        copy.wait_send()


def exchange(kept, counts, decode_slot, queries, keys, values, patch, piece):
    any_space = pl.BlockSpec(memory_space=pl.ANY)
    smem = pl.BlockSpec(memory_space=pltpu.SMEM)
    vmem = pl.BlockSpec(memory_space=pltpu.VMEM)
    return pl.pallas_call(
        exchange_kernel,
        out_shape=(
            jax.ShapeDtypeStruct((192, 128), BF16),
            jax.ShapeDtypeStruct((28, CH, CH), BF16),
        ),
        in_specs=[smem, smem, smem] + [any_space] * 5,
        out_specs=(vmem, any_space),
        scratch_shapes=[
            pltpu.VMEM((8, 256, 256), BF16),
            pltpu.VMEM((8, 256, 256), BF16),
            pltpu.VMEM((8, 256, 256), BF16),
            pltpu.VMEM((2, 2, TILE, HD), BF16),
            pltpu.VMEM((2, NT, TILE, HD), BF16),
            pltpu.VMEM((2, NT, TILE, HD), BF16),
            pltpu.VMEM((256, 256), BF16),
            pltpu.VMEM((64, 256), BF16),
            pltpu.VMEM((2, TILE, 256), BF16),
            pltpu.VMEM((4, 2, 128, 128), BF16),
            pltpu.VMEM((8, 192, 128), BF16),
            pltpu.VMEM((4, 192, 128), BF16),
            pltpu.SemaphoreType.DMA((3, 7)),
            pltpu.SemaphoreType.DMA((3, 8)),
            pltpu.SemaphoreType.DMA((4,)),
            pltpu.SemaphoreType.DMA((4, 2, 3)),
            pltpu.SemaphoreType.DMA((8,)),
            pltpu.SemaphoreType.DMA((3,)),
            pltpu.SemaphoreType.DMA((3,)),
            pltpu.SemaphoreType.DMA,
            pltpu.SemaphoreType.DMA((12,)),
            pltpu.SemaphoreType.DMA((12,)),
        ],
        compiler_params=pltpu.CompilerParams(
            collective_id=0, has_side_effects=True, vmem_limit_bytes=60 << 20
        ),
        cost_estimate=pl.CostEstimate(
            flops=4 * 16 * 4 * 256 * 256 * 128, bytes_accessed=10 << 20, transcendentals=1 << 22
        ),
    )(kept, counts, decode_slot, queries, keys, values, patch, piece)


def slot_of(offset):
    return offset if offset < 21 else offset + 1


def decode_kernel(
    latent, first_kernel, weights, out, window, first, act, weights_vmem, weight_sem
):
    me = lax.axis_index("sp")
    load = pltpu.make_async_copy(weights, weights_vmem, weight_sem)
    load.start()

    twice = (
        lax.broadcasted_iota(jnp.int32, (384, 192), 0) // 2
        == lax.broadcasted_iota(jnp.int32, (384, 192), 1)
    ).astype(BF16)
    doubled = jnp.dot(twice, latent[...], preferred_element_type=F32)
    column = lax.broadcasted_iota(jnp.int32, (384, 128), 0) % 32
    here = jnp.where(column % 2 == 0, doubled, pltpu.roll(doubled, 128 - LAT, axis=1))
    before = jnp.where(column == 0, here, pltpu.roll(here, 1, axis=0))
    after = jnp.where(column == 31, here, pltpu.roll(here, 383, axis=0))
    source_lane = lax.broadcasted_iota(jnp.int32, (384, 512), 0)
    target_lane = lax.broadcasted_iota(jnp.int32, (384, 512), 1)
    slot = target_lane % 128
    wanted = (slot // LAT) * 128 + (target_lane // 128) * 32 + slot % LAT
    pick = jnp.logical_and(slot < 48, source_lane == wanted).astype(BF16)
    joined = jnp.dot(
        jnp.concatenate([before, here, after], axis=1).astype(BF16),
        pick,
        preferred_element_type=F32,
    ).astype(BF16)
    for row in range(6):
        for frame_low in range(2):
            at = (row * 2 + frame_low) * 32
            for frame_high in range(2):
                for up in range(2):
                    lane = (frame_high * 2 + up) * 128
                    window[frame_high * 2 + frame_low, 2 * row + up] = joined[
                        at : at + 32, lane : lane + 128
                    ]

    @pl.when(me == 0)
    def _():
        window[:, 1] = window[:, 2]

    @pl.when(me == 7)
    def _():
        window[:, 10] = window[:, 9]

    wide_column = lax.broadcasted_iota(jnp.int32, (320, CH), 0) % 32
    for frame in range(4):
        total = jnp.zeros((320, CH), F32)
        for time in range(3):
            source = max(frame + time - 2, 0)
            for row in range(3):
                offset = (time * 3 + row) * 48
                total = total + jnp.dot(
                    window[source, row : row + 10, :, 0:48].reshape(320, 48),
                    first_kernel[offset : offset + 48],
                    preferred_element_type=F32,
                )
        rounded = (total * VAE_SCALE).astype(BF16)
        first[frame * 256 : frame * 256 + 256] = rounded[32:288]
        wide = rounded.astype(F32)
        wide = (wide / (1.0 + jnp.exp(-wide))).astype(BF16).astype(F32)
        before = jnp.where(wide_column == 0, wide, pltpu.roll(wide, 1, axis=0))
        after = jnp.where(wide_column == 31, wide, pltpu.roll(wide, 319, axis=0))
        for place, part in enumerate((before, wide, after)):
            part = part.reshape(10, 32, CH).astype(BF16)
            act[frame + 2, :, :, place * CH : place * CH + CH] = part
            if frame == 0:
                act[0, :, :, place * CH : place * CH + CH] = part
                act[1, :, :, place * CH : place * CH + CH] = part

    @pl.when(me == 0)
    def _():
        act[:, 0] = act[:, 1]

    @pl.when(me == 7)
    def _():
        act[:, 9] = act[:, 8]

    load.wait()
    for part in range(2):
        total = first[part * 512 : part * 512 + 512].astype(F32)
        for time in range(3):
            for row in range(3):
                slot = slot_of((time * 3 + row) * 3)
                block = act[part * 2 + time : part * 2 + time + 2, row : row + 8]
                total = total + jnp.dot(
                    block.reshape(512, 3 * CH),
                    weights_vmem[slot : slot + 3].reshape(3 * CH, CH),
                    preferred_element_type=F32,
                )
        out[part * 512 : part * 512 + 512] = total.astype(BF16)


def decode(latent, first_kernel, weights):
    vmem = pl.BlockSpec(memory_space=pltpu.VMEM)
    return pl.pallas_call(
        decode_kernel,
        out_shape=jax.ShapeDtypeStruct((1024, CH), BF16),
        in_specs=[vmem, vmem, pl.BlockSpec(memory_space=pl.ANY)],
        out_specs=vmem,
        scratch_shapes=[
            pltpu.VMEM((4, 12, 32, 128), BF16),
            pltpu.VMEM((1024, CH), BF16),
            pltpu.VMEM((6, 10, 32, 3 * CH), BF16),
            pltpu.VMEM((28, CH, CH), BF16),
            pltpu.SemaphoreType.DMA,
        ],
        compiler_params=pltpu.CompilerParams(vmem_limit_bytes=40 << 20),
        cost_estimate=pl.CostEstimate(
            flops=2 * 1024 * 27 * 256 * 256, bytes_accessed=5 << 20, transcendentals=1 << 19
        ),
    )(latent, first_kernel, weights)


def local(
    queries,
    key_states,
    value_states,
    kept_tiles,
    kept_counts,
    patch_weight,
    decode_slot,
    first_kernel,
    second_kernel,
):
    latent, weights = exchange(
        kept_tiles.transpose(1, 2, 0),
        kept_counts.transpose(1, 0),
        decode_slot,
        queries.reshape(256, HEADS * HD),
        key_states.reshape(256, HEADS * HD),
        value_states.reshape(256, HEADS * HD),
        patch_weight.transpose(1, 0),
        second_kernel,
    )
    decoded = decode(latent, first_kernel.reshape(27 * LAT, CH), weights)
    return decoded.reshape(1, 1, 4, 8, 32, CH)


def solution(mesh):
    tokens = P("segment", "grp", None, "sp", None, None)
    return jax.shard_map(
        local,
        mesh=mesh,
        in_specs=(tokens, tokens, tokens, P(), P(), P(), P(), P(), P(None, "grp", None)),
        out_specs=tokens,
        check_vma=False,
    )
```

time: 332 us -> 110 us (0.33)
  the two profiles are of different devices: /device:TPU:8 before, /device:TPU:1 now
where the time goes in v1:
time: 110 us
  Pallas kernels  107 us (97%)
  local copies, waits for them, and re-layouts  2.83 us (3%)
    pallas_call x1, Pallas kernels, exchange(): pl.pallas_call(exchange_kernel, out_shape=(jax.ShapeDtypeStruct((192, 128...  99.1 us
    pallas_call x1, Pallas kernels, decode(): pl.pallas_call(decode_kernel, out_shape=jax.ShapeDtypeStruct((1024, CH),...  7.68 us
    unnamed x6, local copies, waits for them, and re-layouts  2.83 us

profile of v1, /device:TPU:1, one launch (start us, length us, event | category | flops | bytes accessed | tf_op | source)
XLA Modules:
  0.0 109.6 jit_solution(15526694746521990017)
XLA Ops:
  0.0 0.0 copy-start
  0.0 99.1 %shard_map.91 = (bf16[192,128]{1,0:T(8,128)(2,1)}, bf16[28,256,256]{2,1,0:T(8,128)(2,1)}) custom-call(s32[8,4,16]{2,1,0:T(4,128)} %bitcast.13, s32[8,16]{1,0:T(8,128)} %bitcast.14, s32[4]{0:T(128)} %decode_slot.1, bf16[256,2048]{1,0:T(8,128)(2,1)} %bitcast.9, bf16[256,2048]{1,0:T(8,128)(2,1)} %bitcast.10, bf16[256,2048]{1,0:T(8,128)(2,1)} %bitcast.11, ...), custom_call_target="tpu_custom_call" | custom-call | flops 2147483648 | bytes 10485760 | tf_op jit(solution)/shard_map/pallas_call | solution.py:367
  99.1 0.0 copy-done
  99.1 0.0 copy-start.1
  99.1 2.0 %copy-done.1 = bf16[28,256,256]{2,1,0:T(8,128)(2,1)S(1)} copy-done((bf16[28,256,256]{2,1,0:T(8,128)(2,1)S(1)}, bf16[28,256,256]{2,1,0:T(8,128)(2,1)}, u32[]{:S(2)}) %copy-start.1) | copy-done | bytes 3670040
  101.1 0.0 copy-start.2
  101.1 0.8 copy-done.2
  101.9 7.7 %shard_map.92 = bf16[1024,256]{1,0:T(8,128)(2,1)} custom-call(bf16[192,128]{1,0:T(8,128)(2,1)S(1)} %copy-done.2, bf16[432,256]{1,0:T(8,128)(2,1)S(1)} %bitcast.8, bf16[28,256,256]{2,1,0:T(8,128)(2,1)S(1)} %copy-done.1), custom_call_target="tpu_custom_call" | custom-call | flops 3623878656 | bytes 5242880 | tf_op jit(solution)/shard_map/pallas_call | solution.py:506
Async XLA Ops:
  0.0 99.1 %copy-start = (bf16[27,16,256]{2,1,0:T(8,128)(2,1)S(1)}, bf16[27,16,256]{2,1,0:T(8,128)(2,1)}, u32[]{:S(2)}) copy-start(bf16[27,16,256]{2,1,0:T(8,128)(2,1)} %param.16) | copy-start | bytes 663556
  99.1 2.0 %copy-start.1 = (bf16[28,256,256]{2,1,0:T(8,128)(2,1)S(1)}, bf16[28,256,256]{2,1,0:T(8,128)(2,1)}, u32[]{:S(2)}) copy-start(bf16[28,256,256]{2,1,0:T(8,128)(2,1)} %get-tuple-element.8.weights) | copy-start | bytes 11010052
  101.1 0.8 copy-start.2

commit v2 on v1

--- a/solution.py
+++ b/solution.py
@@ -51,14 +51,20 @@
     tile_k,
     tile_v,
     order,
-    patch_own,
-    attended,
+    patch_all,
+    own_values,
+    projected,
+    packed,
     part_out,
+    sib_in,
+    part_sum,
     part_in,
     seg_latent,
     send_sem,
     recv_sem,
     local_sem,
+    sib_send,
+    sib_recv,
     part_send,
     part_recv,
     seg_send,
@@ -98,6 +104,27 @@
         pl.semaphore_signal(barrier, inc=1, device_id={"grp": peer}, device_id_type=MESH)
     pl.semaphore_wait(barrier, 18)
 
+    sends = []
+
+    def send(a, source, target):
+        for i, peer in enumerate(peers):
+            copy = remote(source(peer), target.at[me], send_sem.at[a, i], recv_sem.at[a, me], sp=peer)
+            copy.start()
+            sends.append(copy)
+
+    def columns_of(ref):
+        return lambda peer: ref.at[:, pl.ds(pl.multiple_of(peer * 256, 256), 256)]
+
+    load_values = pltpu.make_async_copy(values, own_values, local_sem.at[0])
+    load_values.start()
+    load_patch = pltpu.make_async_copy(patch, patch_all, local_sem.at[1])
+    load_patch.start()
+    send(0, columns_of(keys), got_k)
+    keep_keys = pltpu.make_async_copy(columns_of(keys)(me), got_k.at[me], local_sem.at[2])
+    keep_keys.start()
+    keep_queries = pltpu.make_async_copy(columns_of(queries)(me), got_q.at[me], local_sem.at[3])
+    keep_queries.start()
+
     quarter = seg * 7
     taps = pl.ds(quarter, 7)
     lanes = pl.ds(pl.multiple_of(core * 128, 128), 128)
@@ -110,30 +137,29 @@
     )
     w_cross.start()
 
-    arrays = ((keys, got_k), (values, got_v), (queries, got_q))
-    sends = []
-    for a, (source, target) in enumerate(arrays):
-        for i, peer in enumerate(peers):
-            columns = pl.ds(pl.multiple_of(peer * 256, 256), 256)
-            copy = remote(
-                source.at[:, columns],
-                target.at[me],
-                send_sem.at[a, i],
-                recv_sem.at[a, me],
-                sp=peer,
-            )
-            copy.start()
-            sends.append(copy)
-    own_columns = pl.ds(pl.multiple_of(me * 256, 256), 256)
-    keeps = []
-    for a, (source, target) in enumerate(arrays):
-        copy = pltpu.make_async_copy(source.at[:, own_columns], target.at[me], local_sem.at[a])
-        copy.start()
-        keeps.append(copy)
-    patch_copy = pltpu.make_async_copy(
-        patch.at[:, pl.ds(pl.multiple_of(me * 256, 256), 256)], patch_own, local_sem.at[3]
-    )
-    patch_copy.start()
+    load_values.wait()
+    load_patch.wait()
+    patch_lane = lax.broadcasted_iota(jnp.int32, (64, 256), 1)
+
+    def project(peer, carry):
+        columns = pl.ds(pl.multiple_of(peer * 256, 256), 256)
+        weight = patch_all[:, columns].astype(F32)
+        weight = jnp.concatenate(
+            [jnp.where(patch_lane < HD, weight, 0.0), jnp.where(patch_lane < HD, 0.0, weight)],
+            axis=0,
+        ).astype(BF16)
+        projected[peer] = lax.dot_general(
+            own_values[:, columns],
+            weight,
+            (((1,), (1,)), ((), ())),
+            preferred_element_type=F32,
+        ).astype(BF16)
+        return carry
+
+    lax.fori_loop(0, 8, project, 0)
+    send(1, lambda peer: projected.at[peer], got_v)
+    got_v[me] = projected[me]
+    send(2, columns_of(queries), got_q)
 
     w_keep.wait()
     w_cross.wait()
@@ -144,9 +170,45 @@
         copy = remote(block, block, w_send.at[1 + i], w_recv.at[1 + i], grp=peer)
         copy.start()
         y_sends.append(copy)
-    for copy in keeps:
-        copy.wait()
-    patch_copy.wait()
+    keep_keys.wait()
+    keep_queries.wait()
+    def wait_block(a, target, src):
+        remote(
+            target.at[src], target.at[src], send_sem.at[a, 0], recv_sem.at[a, src], sp=sibling
+        ).wait_recv()
+
+    to_row = lax.broadcasted_iota(jnp.int32, (256, 256), 0)
+    from_row = lax.broadcasted_iota(jnp.int32, (256, 256), 1)
+    wanted = ((to_row % 128) // 8) * 16 + (to_row // 128) * 8 + to_row % 8
+    order[...] = (from_row == wanted).astype(BF16)
+
+    def place(got, src, tiles, first_tile):
+        block = jnp.dot(order[...], got[src], preferred_element_type=F32).astype(BF16)
+        rows = pl.ds(pl.multiple_of((src % 2) * 128, 128), 128)
+        for head in range(2):
+            for side in range(2):
+                tiles[head, first_tile + side, rows] = block[
+                    side * 128 : side * 128 + 128, head * 128 : head * 128 + 128
+                ]
+
+    value_lane = lax.broadcasted_iota(jnp.int32, (256, 128), 1)
+
+    def place_keys(src):
+        place(got_k, src, tile_k, 2 * (src // 2))
+        block = jnp.dot(order[...], got_v[src], preferred_element_type=F32)
+        turned = pltpu.roll(block, 64, axis=1)
+        rows = pl.ds(pl.multiple_of((src % 2) * 128, 128), 128)
+        for head, (left, right) in enumerate(((block, turned), (turned, block))):
+            both = jnp.where(value_lane < 64, left, right).astype(BF16)
+            for side in range(2):
+                tile_v[head, 2 * (src // 2) + side, rows] = both[side * 128 : side * 128 + 128]
+
+    place_keys(me)
+    for peer in (peers[6], peers[4], peers[5]):
+        wait_block(0, got_k, peer)
+        wait_block(1, got_v, peer)
+        place_keys(peer)
+
     for copy in y_sends:
         copy.wait()
     x_sends = []
@@ -156,61 +218,18 @@
         copy.start()
         x_sends.append(copy)
 
-    def wait_block(a, target, src):
-        remote(
-            target.at[src], target.at[src], send_sem.at[a, 0], recv_sem.at[a, src], sp=sibling
-        ).wait_recv()
-
-    to_row = lax.broadcasted_iota(jnp.int32, (256, 256), 0)
-    from_row = lax.broadcasted_iota(jnp.int32, (256, 256), 1)
-    wanted = ((to_row % 128) // 8) * 16 + (to_row // 128) * 8 + to_row % 8
-    order[...] = (from_row == wanted).astype(BF16)
-
-    def place(got, src, tiles, first_tile):
-        block = jnp.dot(order[...], got[src], preferred_element_type=F32).astype(BF16)
-        rows = pl.ds(pl.multiple_of((src % 2) * 128, 128), 128)
-        for head in range(2):
-            for side in range(2):
-                tiles[head, first_tile + side, rows] = block[
-                    side * 128 : side * 128 + 128, head * 128 : head * 128 + 128
-                ]
-
-    def place_keys(src):
-        place(got_k, src, tile_k, 2 * (src // 2))
-        place(got_v, src, tile_v, 2 * (src // 2))
-
-    place_keys(me)
-    for peer in (peers[6], peers[4], peers[5]):
-        wait_block(0, got_k, peer)
-        wait_block(1, got_v, peer)
-        place_keys(peer)
-
-    for copy in x_sends:
-        copy.wait()
-    all_lanes = weights_out.at[:, :, lanes]
-    to_sibling = remote(all_lanes, all_lanes, w_send.at[11], w_recv.at[11], sp=sibling)
-    to_sibling.start()
-
     for peer in peers[:4]:
         wait_block(0, got_k, peer)
         wait_block(1, got_v, peer)
         place_keys(peer)
 
     head_base = me * 2
-    zero_patch = jnp.zeros((64, 256), F32)
-    own_patch = patch_own[...].astype(F32)
-    wide_patch = jnp.concatenate(
-        [
-            jnp.concatenate([own_patch, zero_patch], axis=1),
-            jnp.concatenate([zero_patch, own_patch], axis=1),
-        ],
-        axis=0,
-    ).astype(BF16)
+    packed_lane = lax.broadcasted_iota(jnp.int32, (64, 128), 1)
 
     def one_tile(owner, side):
         tile = 2 * owner + side
+        latent = jnp.zeros((TILE, 128), F32)
         for head in range(2):
-            low = head * 128
             query = tile_q[head, side]
             live = counts[tile, head_base + head]
             scores, picks = [], []
@@ -230,7 +249,7 @@
                 top = jnp.maximum(top, jnp.where(slot < live, scores[slot], -1e30))
             top = jnp.max(top, axis=1, keepdims=True) * EXPONENT_SCALE
             total = jnp.zeros((TILE, TILE), F32)
-            result = jnp.zeros((TILE, HD), F32)
+            result = jnp.zeros((TILE, 128), F32)
             for slot in range(KEEP):
                 shift = top if slot == 0 else jnp.where(slot < live, top, 1e30)
                 exponent = jnp.exp2(scores[slot] * EXPONENT_SCALE - shift)
@@ -239,17 +258,31 @@
                     exponent.astype(BF16), tile_v[head, picks[slot]], preferred_element_type=F32
                 )
             total = jnp.sum(total, axis=1, keepdims=True)
-            attended[side, :, low : low + 128] = (result / total).astype(BF16)
-
-    def part_targets(owner, half):
-        block = 2 * owner + half
+            latent = latent + result * (1.0 / total)
+        for half in range(2):
+            base = half * 128
+            packed[side, half] = jnp.where(
+                packed_lane < 64, latent[base : base + 64], latent[base + 64 : base + 128]
+            )
+
+    def part_targets(owner):
+        block = 2 * owner + core
         last = block // 7
         start = 1 - (block + 6) // 7
-        own = part_out.at[owner, half]
+        own = part_sum.at[owner]
         return (
-            (own, block, 32, 128),
-            (own.at[pl.ds(96, 32)], block + 1 - last, 160 * last, 32),
-            (own.at[pl.ds(0, 32)], block - 1 + start, 160 * (1 - start), 32),
+            (own, block, 32, 128, 0),
+            (own.at[pl.ds(96, 32)], block + 1 - last, 160 * last, 32, 1 + last),
+            (own.at[pl.ds(0, 32)], block - 1 + start, 160 * (1 - start), 32, 2 - start),
+        )
+
+    def to_sibling_part(owner):
+        return remote(
+            part_out.at[owner, 1 - core],
+            sib_in.at[owner],
+            sib_send.at[owner],
+            sib_recv.at[owner],
+            sp=sibling,
         )
 
     def one_chip(owner):
@@ -257,56 +290,46 @@
         place(got_q, 2 * owner + 1, tile_q, 0)
         one_tile(owner, 0)
         one_tile(owner, 1)
-        stacked = []
-        for half in range(2):
-            for side in range(2):
-                base = half * 128
-                stacked.append(
-                    jnp.concatenate(
-                        [
-                            attended[side, base : base + 64],
-                            attended[side, base + 64 : base + 128],
-                        ],
-                        axis=1,
-                    )
-                )
-        projected = lax.dot_general(
-            jnp.concatenate(stacked, axis=0),
-            wide_patch,
-            (((1,), (1,)), ((), ())),
-            preferred_element_type=F32,
-        )
         for half in range(2):
             pieces = []
             for row in range(4):
                 for frame in range(2):
                     for side in range(2):
-                        at = ((half * 2 + side) * 8 + frame * 4 + row) * 8
-                        pieces.append(projected[at : at + 8])
+                        at = (frame * 4 + row) * 8
+                        pieces.append(packed[side, half, at : at + 8])
             part_out[owner, half] = jnp.concatenate(pieces, axis=0).astype(BF16)
-        for half in range(2):
-            for kind, (source, target, at, size) in enumerate(part_targets(owner, half)):
-                place_at = part_in.at[me, pl.ds(pl.multiple_of(at, 32), size)]
-
-                @pl.when(target != me)
-                def _():
-                    remote(
-                        source,
-                        place_at,
-                        part_send.at[owner, half, kind],
-                        part_recv.at[me],
-                        sp=target,
-                    ).start()
-
-                @pl.when(target == me)
-                def _():
-                    pltpu.make_async_copy(source, place_at, part_recv.at[me]).start()
+        exchange_parts = to_sibling_part(owner)
+        exchange_parts.start()
+        exchange_parts.wait_recv()
+        part_sum[owner] = (
+            part_out[owner, core].astype(F32) + sib_in[owner].astype(F32)
+        ).astype(BF16)
+        for kind, (source, target, at, size, region) in enumerate(part_targets(owner)):
+            place_at = part_in.at[chip, pl.ds(pl.multiple_of(at, 32), size)]
+            arrived = part_recv.at[chip, region]
+
+            @pl.when(target != me)
+            def _():
+                remote(source, place_at, part_send.at[owner, kind], arrived, sp=target).start()
+
+            @pl.when(target == me)
+            def _():
+                pltpu.make_async_copy(source, place_at, arrived).start()
+
+    all_lanes = weights_out.at[:, :, lanes]
+    to_sibling = remote(all_lanes, all_lanes, w_send.at[11], w_recv.at[11], sp=sibling)
 
     def chip_turn(turn, carry):
         owner = (
             (turn == 0) * chip + (turn == 1) * near + (turn == 2) * far + (turn == 3) * mirror
         )
 
+        @pl.when(turn == 2)
+        def _():
+            for copy in x_sends:
+                copy.wait()
+            to_sibling.start()
+
         @pl.when(turn > 0)
         def _():
             for k in range(2):
@@ -318,10 +341,11 @@
     wait_block(2, got_q, sibling)
     lax.fori_loop(0, 4, chip_turn, 0)
 
-    for src in range(8):
-        pltpu.make_async_copy(part_in.at[src], part_in.at[src], part_recv.at[src]).wait()
     latent = jnp.zeros((192, 128), F32)
-    for src in range(8):
+    for src in range(4):
+        for region, (at, size) in enumerate(((32, 128), (0, 32), (160, 32))):
+            rows = part_in.at[src, pl.ds(at, size)]
+            pltpu.make_async_copy(rows, rows, part_recv.at[src, region]).wait()
         latent = latent + part_in[src].astype(F32)
     seg_latent[seg] = latent.astype(BF16)
     seg_copies = []
@@ -339,18 +363,18 @@
     latent_out[...] = seg_latent[source]
 
     def drain(owner, carry):
-        for half in range(2):
-            for kind, (source, target, at, size) in enumerate(part_targets(owner, half)):
-
-                @pl.when(target != me)
-                def _():
-                    remote(
-                        source,
-                        part_in.at[me, pl.ds(0, size)],
-                        part_send.at[owner, half, kind],
-                        part_recv.at[me],
-                        sp=target,
-                    ).wait_send()
+        to_sibling_part(owner).wait_send()
+        for kind, (source, target, at, size, region) in enumerate(part_targets(owner)):
+
+            @pl.when(target != me)
+            def _():
+                remote(
+                    source,
+                    part_in.at[chip, pl.ds(0, size)],
+                    part_send.at[owner, kind],
+                    part_recv.at[chip, region],
+                    sp=target,
+                ).wait_send()
 
         return carry
 
@@ -375,21 +399,27 @@
         scratch_shapes=[
             pltpu.VMEM((8, 256, 256), BF16),
             pltpu.VMEM((8, 256, 256), BF16),
-            pltpu.VMEM((8, 256, 256), BF16),
+            pltpu.VMEM((8, 256, 128), BF16),
             pltpu.VMEM((2, 2, TILE, HD), BF16),
             pltpu.VMEM((2, NT, TILE, HD), BF16),
-            pltpu.VMEM((2, NT, TILE, HD), BF16),
+            pltpu.VMEM((2, NT, TILE, 128), BF16),
             pltpu.VMEM((256, 256), BF16),
-            pltpu.VMEM((64, 256), BF16),
-            pltpu.VMEM((2, TILE, 256), BF16),
+            pltpu.VMEM((64, HEADS * HD), BF16),
+            pltpu.VMEM((256, HEADS * HD), BF16),
+            pltpu.VMEM((8, 256, 128), BF16),
+            pltpu.VMEM((2, 2, 64, 128), F32),
             pltpu.VMEM((4, 2, 128, 128), BF16),
-            pltpu.VMEM((8, 192, 128), BF16),
+            pltpu.VMEM((4, 128, 128), BF16),
+            pltpu.VMEM((4, 128, 128), BF16),
+            pltpu.VMEM((4, 192, 128), BF16),
             pltpu.VMEM((4, 192, 128), BF16),
             pltpu.SemaphoreType.DMA((3, 7)),
             pltpu.SemaphoreType.DMA((3, 8)),
             pltpu.SemaphoreType.DMA((4,)),
-            pltpu.SemaphoreType.DMA((4, 2, 3)),
-            pltpu.SemaphoreType.DMA((8,)),
+            pltpu.SemaphoreType.DMA((4,)),
+            pltpu.SemaphoreType.DMA((4,)),
+            pltpu.SemaphoreType.DMA((4, 3)),
+            pltpu.SemaphoreType.DMA((4, 3)),
             pltpu.SemaphoreType.DMA((3,)),
             pltpu.SemaphoreType.DMA((3,)),
             pltpu.SemaphoreType.DMA,
@@ -515,7 +545,7 @@
             pltpu.VMEM((28, CH, CH), BF16),
             pltpu.SemaphoreType.DMA,
         ],
-        compiler_params=pltpu.CompilerParams(vmem_limit_bytes=40 << 20),
+        compiler_params=pltpu.CompilerParams(vmem_limit_bytes=60 << 20),
         cost_estimate=pl.CostEstimate(
             flops=2 * 1024 * 27 * 256 * 256, bytes_accessed=5 << 20, transcendentals=1 << 19
         ),

time: 110 us -> 95.6 us (0.87)
  Pallas kernels: 107 us -> 95.1 us
  local copies, waits for them, and re-layouts: 2.83 us -> 0 us
    pallas_call x1, Pallas kernels: 99.1 us -> 86.7 us  [exchange(): pl.pallas_call(exchange_kernel, out_shape=(jax.ShapeDtypeStruct((192, 128...]
    unnamed x6 -> x0, local copies, waits for them, and re-layouts: 2.83 us -> none
where the time goes in v2:
time: 95.6 us; the launch traced here: 95.1 us
  Pallas kernels  95.1 us (99%)
    pallas_call x1, Pallas kernels, exchange(): pl.pallas_call(exchange_kernel, out_shape=(jax.ShapeDtypeStruct((192, 128...  86.7 us
    pallas_call x1, Pallas kernels, decode(): pl.pallas_call(decode_kernel, out_shape=jax.ShapeDtypeStruct((1024, CH),...  8.41 us

profile of v2, /device:TPU:1, one launch (start us, length us, event | category | flops | bytes accessed | tf_op | source)
XLA Modules:
  0.0 95.1 jit_solution(9021793565672896261)
XLA Ops:
  0.0 86.7 %shard_map.91 = (bf16[192,128]{1,0:T(8,128)(2,1)}, bf16[28,256,256]{2,1,0:T(8,128)(2,1)}) custom-call(s32[8,4,16]{2,1,0:T(4,128)} %bitcast.13, s32[8,16]{1,0:T(8,128)} %bitcast.14, s32[4]{0:T(128)} %decode_slot.1, bf16[256,2048]{1,0:T(8,128)(2,1)} %bitcast.8, bf16[256,2048]{1,0:T(8,128)(2,1)} %bitcast.9, bf16[256,2048]{1,0:T(8,128)(2,1)} %bitcast.10, ...), custom_call_target="tpu_custom_call" | custom-call | flops 2147483648 | bytes 10485760 | tf_op jit(solution)/shard_map/pallas_call | solution.py:391
  86.7 8.4 %shard_map.92 = bf16[1024,256]{1,0:T(8,128)(2,1)} custom-call(bf16[192,128]{1,0:T(8,128)(2,1)} %get-tuple-element.7.latent, bf16[432,256]{1,0:T(8,128)(2,1)} %bitcast.12, bf16[28,256,256]{2,1,0:T(8,128)(2,1)} %get-tuple-element.8.weights), custom_call_target="tpu_custom_call" | custom-call | flops 3623878656 | bytes 5242880 | tf_op jit(solution)/shard_map/pallas_call | solution.py:536

commit v3 on v2

--- a/solution.py
+++ b/solution.py
@@ -324,12 +324,6 @@
             (turn == 0) * chip + (turn == 1) * near + (turn == 2) * far + (turn == 3) * mirror
         )
 
-        @pl.when(turn == 2)
-        def _():
-            for copy in x_sends:
-                copy.wait()
-            to_sibling.start()
-
         @pl.when(turn > 0)
         def _():
             for k in range(2):
@@ -340,6 +334,9 @@
 
     wait_block(2, got_q, sibling)
     lax.fori_loop(0, 4, chip_turn, 0)
+    for copy in x_sends:
+        copy.wait()
+    to_sibling.start()
 
     latent = jnp.zeros((192, 128), F32)
     for src in range(4):
@@ -440,7 +437,7 @@
 
 
 def decode_kernel(
-    latent, first_kernel, weights, out, window, first, act, weights_vmem, weight_sem
+    latent, first_kernel, weights, out, window, rows, first, act, weights_vmem, weight_sem
 ):
     me = lax.axis_index("sp")
     load = pltpu.make_async_copy(weights, weights_vmem, weight_sem)
@@ -483,18 +480,19 @@
     def _():
         window[:, 10] = window[:, 9]
 
+    for frame in range(4):
+        rows[frame] = jnp.concatenate(
+            [window[frame, row : row + 10, :, 0:48].reshape(320, 48) for row in range(3)], axis=1
+        )
     wide_column = lax.broadcasted_iota(jnp.int32, (320, CH), 0) % 32
     for frame in range(4):
         total = jnp.zeros((320, CH), F32)
         for time in range(3):
-            source = max(frame + time - 2, 0)
-            for row in range(3):
-                offset = (time * 3 + row) * 48
-                total = total + jnp.dot(
-                    window[source, row : row + 10, :, 0:48].reshape(320, 48),
-                    first_kernel[offset : offset + 48],
-                    preferred_element_type=F32,
-                )
+            total = total + jnp.dot(
+                rows[max(frame + time - 2, 0)],
+                first_kernel[time * 144 : time * 144 + 144],
+                preferred_element_type=F32,
+            )
         rounded = (total * VAE_SCALE).astype(BF16)
         first[frame * 256 : frame * 256 + 256] = rounded[32:288]
         wide = rounded.astype(F32)
@@ -540,6 +538,7 @@
         out_specs=vmem,
         scratch_shapes=[
             pltpu.VMEM((4, 12, 32, 128), BF16),
+            pltpu.VMEM((4, 320, 144), BF16),
             pltpu.VMEM((1024, CH), BF16),
             pltpu.VMEM((6, 10, 32, 3 * CH), BF16),
             pltpu.VMEM((28, CH, CH), BF16),

time: 95.6 us -> 93.2 us (0.975)
  Pallas kernels: 95.1 us -> 92.9 us
    pallas_call x1, Pallas kernels: 86.7 us -> 85.3 us  [exchange(): pl.pallas_call(exchange_kernel, out_shape=(jax.ShapeDtypeStruct((192, 128...]
where the time goes in v3:
time: 93.2 us; the launch traced here: 92.9 us
  Pallas kernels  92.9 us (100%)
    pallas_call x1, Pallas kernels, exchange(): pl.pallas_call(exchange_kernel, out_shape=(jax.ShapeDtypeStruct((192, 128...  85.3 us
    pallas_call x1, Pallas kernels, decode(): pl.pallas_call(decode_kernel, out_shape=jax.ShapeDtypeStruct((1024, CH),...  7.62 us

profile of v3, /device:TPU:1, one launch (start us, length us, event | category | flops | bytes accessed | tf_op | source)
XLA Modules:
  0.0 92.9 jit_solution(14677309535601040054)
XLA Ops:
  0.0 85.3 %shard_map.91 = (bf16[192,128]{1,0:T(8,128)(2,1)}, bf16[28,256,256]{2,1,0:T(8,128)(2,1)}) custom-call(s32[8,4,16]{2,1,0:T(4,128)} %bitcast.13, s32[8,16]{1,0:T(8,128)} %bitcast.14, s32[4]{0:T(128)} %decode_slot.1, bf16[256,2048]{1,0:T(8,128)(2,1)} %bitcast.8, bf16[256,2048]{1,0:T(8,128)(2,1)} %bitcast.9, bf16[256,2048]{1,0:T(8,128)(2,1)} %bitcast.10, ...), custom_call_target="tpu_custom_call" | custom-call | flops 2147483648 | bytes 10485760 | tf_op jit(solution)/shard_map/pallas_call | solution.py:388
  85.3 7.6 %shard_map.92 = bf16[1024,256]{1,0:T(8,128)(2,1)} custom-call(bf16[192,128]{1,0:T(8,128)(2,1)} %get-tuple-element.7.latent, bf16[432,256]{1,0:T(8,128)(2,1)} %bitcast.12, bf16[28,256,256]{2,1,0:T(8,128)(2,1)} %get-tuple-element.8.weights), custom_call_target="tpu_custom_call" | custom-call | flops 3623878656 | bytes 5242880 | tf_op jit(solution)/shard_map/pallas_call | solution.py:534

commit v4 on v3

--- a/solution.py
+++ b/solution.py
@@ -100,9 +100,43 @@
         pl.semaphore_signal(barrier, inc=1, device_id={"sp": peer}, device_id_type=MESH)
     for peer in x_peers:
         pl.semaphore_signal(barrier, inc=1, device_id={"segment": peer}, device_id_type=MESH)
-    for peer in [z_partner] + y_peers:
+    for peer in y_peers:
         pl.semaphore_signal(barrier, inc=1, device_id={"grp": peer}, device_id_type=MESH)
-    pl.semaphore_wait(barrier, 18)
+    at_border = chip % 3 == 0
+    source_chip = 3 * (1 - chip // 2)
+    pl.semaphore_signal(
+        barrier,
+        inc=1,
+        device_id={"grp": z_partner, "sp": source_chip * 2 + core},
+        device_id_type=MESH,
+    )
+    pl.semaphore_wait(barrier, 17 + 2 * at_border.astype(jnp.int32))
+
+    quarter = seg * 7
+    taps = pl.ds(quarter, 7)
+    lanes = pl.ds(pl.multiple_of(core * 128, 128), 128)
+    own_part = piece.at[pl.ds(quarter - seg // 3, 7), :, lanes]
+    own_rows = pl.ds(pl.multiple_of(grp * 16, 16), 16)
+    own_place = weights_out.at[taps, own_rows, lanes]
+    w_keep = pltpu.make_async_copy(own_part, own_place, w_local)
+    w_keep.start()
+    beyond = mirror + 1 - 2 * (mirror % 2)
+    w_cross = [
+        remote(
+            own_part,
+            own_place,
+            w_send.at[place],
+            w_recv.at[0],
+            grp=z_partner,
+            sp=target * 2 + core,
+        )
+        for place, target in ((0, mirror), (12, beyond))
+    ]
+
+    @pl.when(at_border)
+    def _():
+        for copy in w_cross:
+            copy.start()
 
     sends = []
 
@@ -124,18 +158,6 @@
     keep_keys.start()
     keep_queries = pltpu.make_async_copy(columns_of(queries)(me), got_q.at[me], local_sem.at[3])
     keep_queries.start()
-
-    quarter = seg * 7
-    taps = pl.ds(quarter, 7)
-    lanes = pl.ds(pl.multiple_of(core * 128, 128), 128)
-    own_part = piece.at[pl.ds(quarter - seg // 3, 7), :, lanes]
-    own_rows = pl.ds(pl.multiple_of(grp * 16, 16), 16)
-    w_keep = pltpu.make_async_copy(own_part, weights_out.at[taps, own_rows, lanes], w_local)
-    w_keep.start()
-    w_cross = remote(
-        own_part, weights_out.at[taps, own_rows, lanes], w_send.at[0], w_recv.at[0], grp=z_partner
-    )
-    w_cross.start()
 
     load_values.wait()
     load_patch.wait()
@@ -162,7 +184,13 @@
     send(2, columns_of(queries), got_q)
 
     w_keep.wait()
-    w_cross.wait()
+    w_cross[0].wait_recv()
+
+    @pl.when(at_border)
+    def _():
+        for copy in w_cross:
+            copy.wait_send()
+
     pair_rows = pl.ds(pl.multiple_of((grp // 2) * 32, 32), 32)
     y_sends = []
     for i, peer in enumerate(y_peers):
@@ -420,7 +448,7 @@
             pltpu.SemaphoreType.DMA((3,)),
             pltpu.SemaphoreType.DMA((3,)),
             pltpu.SemaphoreType.DMA,
-            pltpu.SemaphoreType.DMA((12,)),
+            pltpu.SemaphoreType.DMA((13,)),
             pltpu.SemaphoreType.DMA((12,)),
         ],
         compiler_params=pltpu.CompilerParams(

time: 93.2 us -> 89.9 us (0.965)
  Pallas kernels: 92.9 us -> 89.6 us
    pallas_call x1, Pallas kernels: 85.3 us -> 82 us  [exchange(): pl.pallas_call(exchange_kernel, out_shape=(jax.ShapeDtypeStruct((192, 128...]
where the time goes in v4:
time: 89.9 us; the launch traced here: 89.6 us
  Pallas kernels  89.6 us (100%)
    pallas_call x1, Pallas kernels, exchange(): pl.pallas_call(exchange_kernel, out_shape=(jax.ShapeDtypeStruct((192, 128...  82 us
    pallas_call x1, Pallas kernels, decode(): pl.pallas_call(decode_kernel, out_shape=jax.ShapeDtypeStruct((1024, CH),...  7.62 us

profile of v4, /device:TPU:1, one launch (start us, length us, event | category | flops | bytes accessed | tf_op | source)
XLA Modules:
  0.0 89.6 jit_solution(7288237750221151512)
XLA Ops:
  0.0 82.0 %shard_map.91 = (bf16[192,128]{1,0:T(8,128)(2,1)}, bf16[28,256,256]{2,1,0:T(8,128)(2,1)}) custom-call(s32[8,4,16]{2,1,0:T(4,128)} %bitcast.13, s32[8,16]{1,0:T(8,128)} %bitcast.14, s32[4]{0:T(128)} %decode_slot.1, bf16[256,2048]{1,0:T(8,128)(2,1)} %bitcast.8, bf16[256,2048]{1,0:T(8,128)(2,1)} %bitcast.9, bf16[256,2048]{1,0:T(8,128)(2,1)} %bitcast.10, ...), custom_call_target="tpu_custom_call" | custom-call | flops 2147483648 | bytes 10485760 | tf_op jit(solution)/shard_map/pallas_call | solution.py:416
  82.0 7.6 %shard_map.92 = bf16[1024,256]{1,0:T(8,128)(2,1)} custom-call(bf16[192,128]{1,0:T(8,128)(2,1)} %get-tuple-element.7.latent, bf16[432,256]{1,0:T(8,128)(2,1)} %bitcast.12, bf16[28,256,256]{2,1,0:T(8,128)(2,1)} %get-tuple-element.8.weights), custom_call_target="tpu_custom_call" | custom-call | flops 3623878656 | bytes 5242880 | tf_op jit(solution)/shard_map/pallas_call | solution.py:562

commit v5 on v4

--- a/solution.py
+++ b/solution.py
@@ -83,10 +83,10 @@
     mirror = 3 - chip
     near = chip + 1 - 2 * (chip % 2)
     peers = [
+        mirror * 2 + core,
+        mirror * 2 + 1 - core,
         far * 2 + core,
         far * 2 + 1 - core,
-        mirror * 2 + core,
-        mirror * 2 + 1 - core,
         near * 2 + core,
         near * 2 + 1 - core,
         sibling,
@@ -349,7 +349,7 @@
 
     def chip_turn(turn, carry):
         owner = (
-            (turn == 0) * chip + (turn == 1) * near + (turn == 2) * far + (turn == 3) * mirror
+            (turn == 0) * chip + (turn == 1) * near + (turn == 2) * mirror + (turn == 3) * far
         )
 
         @pl.when(turn > 0)

time: 89.9 us -> 90 us (level)
  no operation moved by 1% of the time
where the time goes in v5:
time: 90 us; the launch traced here: 89.7 us
  Pallas kernels  89.7 us (100%)
    pallas_call x1, Pallas kernels, exchange(): pl.pallas_call(exchange_kernel, out_shape=(jax.ShapeDtypeStruct((192, 128...  82.1 us
    pallas_call x1, Pallas kernels, decode(): pl.pallas_call(decode_kernel, out_shape=jax.ShapeDtypeStruct((1024, CH),...  7.62 us

profile of v5, /device:TPU:1, one launch (start us, length us, event | category | flops | bytes accessed | tf_op | source)
XLA Modules:
  0.0 89.7 jit_solution(13400258534956103417)
XLA Ops:
  0.0 82.1 %shard_map.91 = (bf16[192,128]{1,0:T(8,128)(2,1)}, bf16[28,256,256]{2,1,0:T(8,128)(2,1)}) custom-call(s32[8,4,16]{2,1,0:T(4,128)} %bitcast.13, s32[8,16]{1,0:T(8,128)} %bitcast.14, s32[4]{0:T(128)} %decode_slot.1, bf16[256,2048]{1,0:T(8,128)(2,1)} %bitcast.8, bf16[256,2048]{1,0:T(8,128)(2,1)} %bitcast.9, bf16[256,2048]{1,0:T(8,128)(2,1)} %bitcast.10, ...), custom_call_target="tpu_custom_call" | custom-call | flops 2147483648 | bytes 10485760 | tf_op jit(solution)/shard_map/pallas_call | solution.py:416
  82.1 7.6 %shard_map.92 = bf16[1024,256]{1,0:T(8,128)(2,1)} custom-call(bf16[192,128]{1,0:T(8,128)(2,1)} %get-tuple-element.7.latent, bf16[432,256]{1,0:T(8,128)(2,1)} %bitcast.12, bf16[28,256,256]{2,1,0:T(8,128)(2,1)} %get-tuple-element.8.weights), custom_call_target="tpu_custom_call" | custom-call | flops 3623878656 | bytes 5242880 | tf_op jit(solution)/shard_map/pallas_call | solution.py:562
